TPU v7x, 256 devices: a whole 4x4x8 slice. The times are simulated.
256 devices in a mesh: grp: 16 (over z, core), sub: 16 (over y, x).
Axes of the slice: x: 4, y: 4, z: 8, core: 2. Of those that a mesh axis runs over, the one named last changes fastest.
Arguments:
- macro_state: float32 [1024, 256, 256], P('grp', 'sub'), may hold values from 0 to 6, as said below
- macro_sizes: int32 [1024], replicated, may hold values from 64 to 256
- block_sources: int32 [1024, 4], replicated, may hold values from 0 to 1023, as said below
- event_rates: float32 [1024, 4], P('grp'), may hold values from 0.1 to 1
- first_factor: float32 [4, 256, 256], replicated, may hold values from 0 to 0.015625
- first_pattern: int32 [4, 16, 16], replicated, may hold values 0 or 1
- second_factor: float32 [4, 256, 256], replicated, may hold values from 0 to 0.015625
- second_pattern: int32 [4, 16, 16], replicated, may hold values 0 or 1
Outputs:
- next_state: float32 [1024, 256, 256], P('grp', 'sub')
- growth: float32 [], replicated
Inputs may be any that keep to these rules, and one draw needn't show every extreme that they name: `block_sources`: among the 256 blocks of the macro states of one group, at most 24 name source macro states of any one group, and in every group exactly 24 name some one group. `macro_state`: Positive.
All inputs are finite; a program needn't handle non-finite values.
Results may differ from a plain program's by a relative error of at most 0.00007.
Values sent between devices are 32-bit elements; how exact they have to be, the bound alone decides.
A program may use at most 64 MiB of HBM per device.

v0:
```python
import jax
import jax.numpy as jnp
from jax import lax
from jax.sharding import PartitionSpec as P

highest = lax.Precision.HIGHEST


def expand(values, pattern):
    factor_blocks = pattern.shape[1]
    block_size = values.shape[1] // factor_blocks
    widened = jnp.repeat(
        jnp.repeat(pattern.astype(jnp.float32), block_size, axis=1), block_size, axis=2
    )
    return values * widened


def on_device(
    macro_state,
    macro_sizes,
    block_sources,
    event_rates,
    first_factor,
    first_pattern,
    second_factor,
    second_pattern,
):
    local_macros, local_rows, order = macro_state.shape
    num_events = block_sources.shape[1]
    num_groups = lax.axis_size("grp")
    my_group = lax.axis_index("grp")
    my_piece = lax.axis_index("sub")
    capacity = 6 * local_macros // num_groups
    row_index = my_piece * local_rows + lax.iota(jnp.int32, local_rows)
    own_sizes = lax.dynamic_slice_in_dim(macro_sizes, my_group * local_macros, local_macros)
    alive = (row_index[None, :] < own_sizes[:, None]).astype(jnp.float32)
    masked = macro_state * alive[:, :, None]
    first = expand(first_factor, first_pattern)
    second = expand(second_factor, second_pattern)
    wanted = block_sources.reshape(num_groups, local_macros * num_events)
    from_group = wanted // local_macros
    onehot = (from_group[:, :, None] == lax.iota(jnp.int32, num_groups)[None, None, :]).astype(
        jnp.int32
    )
    slot_index = jnp.sum(onehot * (jnp.cumsum(onehot, axis=1) - 1), axis=2)
    target_slot = jnp.where(from_group == my_group, slot_index, capacity)
    dest_groups = jnp.broadcast_to(lax.iota(jnp.int32, num_groups)[:, None], wanted.shape)
    send_index = (
        jnp.zeros((num_groups, capacity), jnp.int32)
        .at[dest_groups, target_slot]
        .set(wanted - my_group * local_macros, mode="drop")
    )
    outgoing = masked[send_index]
    incoming = lax.all_to_all(outgoing, "grp", split_axis=0, concat_axis=0, tiled=True)
    my_from = lax.dynamic_index_in_dim(from_group, my_group, 0, keepdims=False)
    my_slots = lax.dynamic_index_in_dim(slot_index, my_group, 0, keepdims=False)
    stacked = incoming.reshape(num_groups * capacity, local_rows, order)
    gathered = stacked[my_from * capacity + my_slots].reshape(
        local_macros, num_events, local_rows, order
    )
    scaled = (
        jnp.einsum("mkrc,kdc->mkrd", gathered, second, precision=highest)
        * event_rates[:, :, None, None]
    )
    my_columns = lax.dynamic_slice_in_dim(first, my_piece * local_rows, local_rows, 2)
    summed = lax.psum_scatter(
        jnp.einsum("kar,mkrc->amc", my_columns, scaled, precision=highest),
        "sub",
        scatter_dimension=0,
        tiled=True,
    )
    result = jnp.transpose(summed, (1, 0, 2))
    product = result * alive[:, :, None]
    total, mass = lax.psum((jnp.sum(product), jnp.sum(masked)), ("grp", "sub"))
    live_count = order * jnp.sum(macro_sizes).astype(jnp.float32)
    return (product * (live_count / total), total / mass)


def solution(mesh):
    return jax.shard_map(
        on_device,
        mesh=mesh,
        in_specs=(P("grp", "sub", None), P(), P(), P("grp", None), P(), P(), P(), P()),
        out_specs=(P("grp", "sub", None), P()),
        check_vma=False,
    )
```

profile of v0, /device:TPU:8, one launch (start us, length us, event | category | flops | bytes accessed | tf_op | source)
XLA Modules:
  0.0 420.3 jit_solution(9651238342386669444)
XLA Ops:
  7.2 1.1 copy.29
  8.3 0.3 reshape.233
  8.6 0.3 reshape.234
  8.9 0.3 reshape.232
  9.3 9.1 %reduce-window.6 = s32[16,16,2,128]{3,1,2,0:T(8,128)S(1)} reduce-window(s32[16,16,2,128]{3,1,2,0:T(8,128)S(1)} %fusion.7, s32[]{:T(128)} %constant.20.clone.1), window={size=1x1x1x128 pad=0_0x0_0x0_0x127_0}, to_apply=%region_0.1 | reduce-window | flops 8323072 | bytes 524292 | tf_op jit(solution)/shard_map/reduce-window
  18.5 0.3 copy.32
  19.3 15.5 %scatter_custom_fusion = s32[384]{0:T(512)S(1)} fusion(s32[4096]{0:T(1024)S(1)} %bitcast.67, s32[4096]{0:T(1024)S(1)} %bitcast.68, s32[]{:T(128)} %constant.20.clone.1), kind=kCustom, calls=%fused_computation.55 | custom fusion | bytes 1540
  35.2 0.9 fusion.20
  36.2 3.8 gather_fusion
  40.0 8.7 %all-to-all-start = ((f32[16,24,16,256]{3,2,1,0:T(8,128)}), f32[16,24,16,256]{3,2,1,0:T(8,128)}, u32[]{:S(2)}, u32[]{:S(2)}) async-start(f32[16,24,16,256]{3,2,1,0:T(8,128)} %bitcast.64), calls=%async_computation | async-start | bytes 12582912 | tf_op jit(solution)/shard_map/all_to_all | solution.py:54
  48.8 0.2 reduce-scatter.2.cloned.1.call-start
  49.0 0.3 copy.27
  49.7 0.2 reshape.230
  49.9 0.2 constant_dynamic-slice_fusion
  50.6 0.2 reshape.228
  51.1 136.9 %all-to-all-done = f32[16,24,16,256]{3,2,1,0:T(8,128)} async-done(((f32[16,24,16,256]{3,2,1,0:T(8,128)}), f32[16,24,16,256]{3,2,1,0:T(8,128)}, u32[]{:S(2)}, u32[]{:S(2)}) %all-to-all-start) | async-done | bytes 6291488 | tf_op jit(solution)/shard_map/all_to_all | solution.py:54
  188.0 5.6 %gather_fusion.1 = f32[256,16,256]{2,1,0:T(8,128)} fusion(f32[384,16,256]{2,1,0:T(8,128)} %bitcast.8, s32[1024]{0:T(1024)S(1)} %pad_clamp_fusion), kind=kCustom, calls=%fused_computation.1 | custom fusion | bytes 8389632 | tf_op jit(solution)/shard_map/gather | solution.py:58
  193.7 5.5 %fusion.1 = f32[4,256,64,16]{1,3,0,2:T(8,128)S(1)} fusion(f32[64,4,16,256]{3,2,1,0:T(8,128)} %bitcast.65, f32[4,256,256]{1,2,0:T(8,128)S(1)} %bitcast_multiply_fusion.3), kind=kOutput, calls=%fused_computation.7 | convolution fusion | flops 3221225472 | bytes 9437184 | tf_op jit(solution)/shard_map/mkrc,kdc->mkrd/dot_general | solution.py:62
  199.3 16.2 %convolution_bitcast_fusion = f32[256,64,256]{2,0,1:T(8,128)} fusion(f32[4,256,64,16]{1,3,0,2:T(8,128)S(1)} %fusion.1, f32[64,4]{1,0:T(8,128)S(1)} %copy.36, f32[4,256,16]{1,2,0:T(8,128)S(1)} %copy.40, f32[4,256,256]{1,2,0:T(8,128)S(1)} %bitcast.66, s32[]{:T(128)S(6)} %select_n.67), kind=kOutput, calls=%fused_computation.3 | convolution fusion | flops 3222290432 | bytes 21135364 | tf_op jit(solution)/shard_map/kar,mkrc->amc/dot_general | solution.py:67
  215.5 0.6 reduce_sum.40
  216.8 113.3 %reduce-scatter.2.cloned.1.call-done = f32[16,64,256]{2,0,1:T(8,128)} async-done(((f32[256,64,256]{2,0,1:T(8,128)}), f32[16,64,256]{2,0,1:T(8,128)}) %reduce-scatter.2.cloned.1.call-update) | async-done | bytes 1048592 | tf_op jit(solution)/shard_map/reduce_scatter | solution.py:66
  330.0 2.2 fusion.4
  332.2 75.6 %all-reduce = (f32[]{:T(128)}, f32[]{:T(128)}) all-reduce(f32[]{:T(128)} %fusion.4, f32[]{:T(128)} %get-tuple-element.4), channel_id=1, replica_groups=mesh['grp'=16,'sub'=16] {'grp','sub'}, use_global_device_ids=true, to_apply=%region_7.8 | all-reduce | flops 2 | bytes 16 | tf_op jit(solution)/shard_map/psum | solution.py:74
  409.9 2.4 fusion.3
  (54 shorter events, 2.1 us)
Async XLA Ops:
  7.2 42.7 %copy-start = (f32[4,256,256]{2,1,0:T(8,128)S(1)}, f32[4,256,256]{2,1,0:T(8,128)}, u32[]{:S(2)}) copy-start(f32[4,256,256]{2,1,0:T(8,128)} %param.12) | copy-start | bytes 3145732
  7.2 11.9 %copy-start.8 = (s32[2]{0:T(128)S(1)}, s32[2]{0:T(128)}, u32[]{:S(2)}) copy-start(s32[2]{0:T(128)} %constant.59) | copy-start | bytes 28
  7.2 11.9 %copy-start.7 = (s32[2]{0:T(128)S(1)}, s32[2]{0:T(128)}, u32[]{:S(2)}) copy-start(s32[2]{0:T(128)} %constant.62) | copy-start | bytes 28
  7.2 27.8 %copy-start.5 = (s32[1024]{0:T(1024)S(1)}, s32[1024]{0:T(1024)}, u32[]{:S(2)}) copy-start(s32[1024]{0:T(1024)} %param.9) | copy-start | bytes 12292
  7.2 28.0 %copy-start.1 = (f32[64,16,256]{2,1,0:T(8,128)S(1)}, f32[64,16,256]{2,1,0:T(8,128)}, u32[]{:S(2)}) copy-start(f32[64,16,256]{2,1,0:T(8,128)} %param.8) | copy-start | bytes 3145732
  40.0 9.0 %copy-start.2 = (f32[4,256,256]{2,1,0:T(8,128)S(1)}, f32[4,256,256]{2,1,0:T(8,128)}, u32[]{:S(2)}) copy-start(f32[4,256,256]{2,1,0:T(8,128)} %param.14) | copy-start | bytes 3145732
  40.0 9.4 %copy-start.3 = (s32[4,16,16]{2,1,0:T(8,128)S(1)}, s32[4,16,16]{2,1,0:T(8,128)}, u32[]{:S(2)}) copy-start(s32[4,16,16]{2,1,0:T(8,128)} %param.15) | copy-start | bytes 12292
  40.0 148.0 %all-to-all-start = ((f32[16,24,16,256]{3,2,1,0:T(8,128)}), f32[16,24,16,256]{3,2,1,0:T(8,128)}, u32[]{:S(2)}, u32[]{:S(2)}) async-start(f32[16,24,16,256]{3,2,1,0:T(8,128)} %bitcast.64), calls=%async_computation | async-start | bytes 12582912 | tf_op jit(solution)/shard_map/all_to_all | solution.py:54
  48.8 1.5 copy-start.4
  48.8 2.1 copy-start.6
  48.8 281.3 %reduce-scatter.2.cloned.1.call-start = ((), (), s32[]{:S(2)}) async-start(), calls=%async_computation.2 | async-start | bytes 17825792 | tf_op jit(solution)/shard_map/reduce_scatter | solution.py:66
Sparse Core Ops, SparseCore 0:
  215.6 114.4 reduce-scatter.1
where the time goes:
time: 422 us; the launch traced here: 420 us
  waiting for transfers between devices  250 us (59%)
  blocking collectives  75.6 us (18%)
  local copies, waits for them, and re-layouts  29.6 us (7%)
  matrix products  21.7 us (5%)
  between operations  18.2 us (4%)
  other arithmetic  15.9 us (4%)
  starting transfers between devices  8.97 us (2%)
    all_to_all x1, waiting for transfers between devices, on_device(): lax.all_to_all(outgoing, 'grp', split_axis=0, concat_axis=0, tiled=True)  137 us
    reduce_scatter x1, waiting for transfers between devices, on_device(): lax.psum_scatter(jnp.einsum('kar,mkrc->amc', my_columns, scaled, precisio...  113 us
    psum x1, blocking collectives, on_device(): total, mass = lax.psum((jnp.sum(product), jnp.sum(masked)), ('grp', 'sub'))  75.6 us
    unnamed x25, local copies, waits for them, and re-layouts  17.2 us
    dot_general x1, matrix products, on_device(): jnp.einsum('kar,mkrc->amc', my_columns, scaled, precision=highest)  16.2 us
    another operation x2, other arithmetic  9.14 us
    all_to_all x1, starting transfers between devices, on_device(): lax.all_to_all(outgoing, 'grp', split_axis=0, concat_axis=0, tiled=True)  8.75 us
  transfers between devices with their start and end apart: 2, of which 2 were waited for; matrix products, arithmetic and copies ran while one was open for 1% of the time, Pallas kernels for 0%

commit v1 on v0

v1 whole, which is shorter than its diff:
```python
import jax
import jax.numpy as jnp
from jax import lax
from jax.experimental import pallas as pl
from jax.experimental.pallas import tpu as pltpu
from jax.sharding import PartitionSpec as P

MESH = pl.DeviceIdType.MESH
F32, BF16 = jnp.float32, jnp.bfloat16
NS = 256
EVENTS = 4
NZ = 8
NSUB = 16
MAC = 64
OWN = MAC // NSUB
BLK = OWN * EVENTS
GROUPS = 2 * NZ
HALF = MAC // 2
CHUNKS = 4
CW, CCW = 0, 1


def split(x):
    high = x.astype(BF16)
    return high, (x - high.astype(F32)).astype(BF16)


def dot(a, b):
    return jnp.dot(a, b, preferred_element_type=F32)


def kernel(
    state_ref, sizes_ref, sizes_vec_ref, sources_ref, rates_ref, first_ref, fpat_ref, second_ref, spat_ref,
    out_ref, stats_ref,
    g0, g1, g2, g3, sb0, sb1, sb2, sb3, rb0, rb1, rb2, rb3,
    fh, fl, stc, zacc, zh, zl, pacc, pb, sums, tsub, tgrp,
    ring_send, ring_recv, d2d_send, d2d_recv, xy_send, xy_recv, tot_send, tot_recv, out_send, out_recv,
):
    gathered, outgo, income = (g0, g1, g2, g3), (sb0, sb1, sb2, sb3), (rb0, rb1, rb2, rb3)
    group, piece = lax.axis_index("grp"), lax.axis_index("sub")
    z, core = group // 2, group % 2
    y, x = piece // 4, piece % 4
    sibling = z * 2 + (1 - core)

    def ring_group(distance):
        return ((z + distance + NZ) % NZ) * 2 + core

    def sub_peer(offset):
        return ((y + offset // 4) % 4) * 4 + (x + offset % 4) % 4

    barrier = pltpu.get_barrier_semaphore()

    @pl.loop(1, NSUB)
    def _(offset):
        pl.semaphore_signal(barrier, inc=1, device_id=(group, sub_peer(offset)), device_id_type=MESH)

    @pl.loop(1, GROUPS)
    def _(offset):
        pl.semaphore_signal(barrier, inc=1, device_id=((group + offset) % GROUPS, piece), device_id_type=MESH)

    row_iota = lax.broadcasted_iota(jnp.int32, (8, 128), 0)

    def stage(q, mass):
        rh, ch = q // 2, q % 2
        rows = row_iota + (piece * 16 + rh * 8)

        def body(m, mass):
            tile = state_ref[m, pl.ds(8 * rh, 8), pl.ds(128 * ch, 128)]
            tile = jnp.where(rows < sizes_ref[group * MAC + m], tile, 0.0)
            gathered[q][group * MAC + m] = tile
            return mass + tile

        return lax.fori_loop(0, MAC, body, mass, unroll=8)

    def ring_piece(q, distance, h):
        return gathered[q].at[pl.ds(ring_group(distance) * MAC + HALF * h, HALF)]

    def ring_copy(q, way, t, h):
        sign = -1 if way == CW else 1
        part = ring_piece(q, sign * (t - 1), h)
        return pltpu.make_async_remote_copy(
            src_ref=part,
            dst_ref=part,
            send_sem=ring_send.at[q],
            recv_sem=ring_recv.at[((q * 2 + way) * 4 + t - 1) * 2 + h],
            device_id=(ring_group(-sign), piece),
            device_id_type=MESH,
        )

    def ring_wait(q, way, t, h):
        sign = -1 if way == CW else 1
        part = ring_piece(q, sign * t, h)
        pltpu.make_async_copy(part, part, ring_recv.at[((q * 2 + way) * 4 + t - 1) * 2 + h]).wait()

    def sibling_copy(q, part):
        pltpu.make_async_remote_copy(
            src_ref=part,
            dst_ref=part,
            send_sem=d2d_send.at[q],
            recv_sem=d2d_recv.at[q],
            device_id=(sibling, piece),
            device_id_type=MESH,
        ).start()

    def carried(way, t):
        return (0, 1) if t < 4 else ((0,) if way == CW else (1,))

    def ring_start(q):
        for h in (0, 1):
            for way in (CW, CCW):
                ring_copy(q, way, 1, h).start()
        sibling_copy(q, gathered[q].at[pl.ds(group * MAC, MAC)])

    def ring_step(q, t):
        for h in (0, 1):
            for way in (CW, CCW):
                if h in carried(way, t):
                    ring_wait(q, way, t, h)
                    if t < 4 and h in carried(way, t + 1):
                        ring_copy(q, way, t + 1, h).start()
                    sibling_copy(q, ring_piece(q, -t if way == CW else t, h))

    def prepare(k):
        rows_of = (lax.broadcasted_iota(jnp.int32, (NS, 16), 0) // 16 == lax.broadcasted_iota(jnp.int32, (NS, 16), 1))
        cols_of = (lax.broadcasted_iota(jnp.int32, (16, NS), 1) // 16 == lax.broadcasted_iota(jnp.int32, (16, NS), 0))
        rows_of, cols_of = rows_of.astype(F32).astype(BF16), cols_of.astype(F32).astype(BF16)

        def widen(pattern):
            return dot(dot(rows_of, pattern.astype(F32).astype(BF16)).astype(BF16), cols_of)

        source = lax.broadcasted_iota(jnp.int32, (NS, NS), 0)
        target = lax.broadcasted_iota(jnp.int32, (NS, NS), 1)
        place = (source // 8 % 2) * 128 + (source // 16) * 8 + source % 8
        order = (place == target).astype(F32).astype(BF16)
        high, low = split(first_ref[k] * widen(fpat_ref[k]))
        for part, dest in ((high, fh), (low, fl)):
            moved = dot(part, order).astype(BF16)
            for rh in (0, 1):
                dest[rh, :, k * 128 : (k + 1) * 128] = moved[:, rh * 128 : (rh + 1) * 128]
        high, low = split((second_ref[k] * widen(spat_ref[k])).T)
        for ch in (0, 1):
            rows = slice(ch * 128, ch * 128 + 128)
            stc[k, ch, 0:128, :] = high[rows]
            stc[k, ch, 128:256, :] = low[rows]
            stc[k, ch, 256:384, :] = high[rows]

    def select(q):
        pltpu.make_async_copy(
            gathered[q].at[pl.ds(0, 512)], gathered[q].at[pl.ds(0, 512)], d2d_recv.at[q]
        ).wait()

        def pick(j, dest, at):
            tiles = [
                gathered[q][sources_ref[k, group * MAC + j * OWN + mm]] for k in range(EVENTS) for mm in range(OWN)
            ]
            for b, tile in enumerate(tiles):
                dest[at, b] = tile

        @pl.loop(1, NSUB)
        def _(offset):
            j = sub_peer(offset)
            pick(j, outgo[q], j)
            pltpu.make_async_remote_copy(
                src_ref=outgo[q].at[j],
                dst_ref=income[q].at[piece],
                send_sem=xy_send.at[q],
                recv_sem=xy_recv.at[q],
                device_id=(group, j),
                device_id_type=MESH,
            ).start()

        pick(piece, income[q], piece)

    def stage1(q):
        rh, ch = q // 2, q % 2
        pltpu.make_async_copy(
            income[q].at[pl.ds(0, NSUB - 1)], income[q].at[pl.ds(0, NSUB - 1)], xy_recv.at[q]
        ).wait()
        for k in range(EVENTS):
            block = income[q][:, k * OWN : (k + 1) * OWN].reshape(NSUB * OWN * 8, 128)
            high, low = split(block)
            part = dot(jnp.concatenate([high, high, low], axis=1), stc[k, ch])
            if ch == 0:
                zacc[k] = part
            else:
                part = (part + zacc[k]).reshape(NSUB, OWN, 8, NS)
                for mm in range(OWN):
                    rate = rates_ref[k, piece * OWN + mm]
                    high, low = split(part[:, mm].reshape(128, NS) * rate)
                    zh[mm, k * 128 : (k + 1) * 128, :] = high
                    zl[mm, k * 128 : (k + 1) * 128, :] = low

    def stage2(mm, rh):
        high, low = zh[mm], zl[mm]
        return dot(fh[rh], high) + dot(fh[rh], low) + dot(fl[rh], high)

    mass = stage(0, jnp.zeros((8, 128), F32))
    pl.semaphore_wait(barrier, NSUB - 1 + GROUPS - 1)
    ring_start(0)
    for q in range(1, CHUNKS):
        mass = stage(q, mass)
    sums[1] = mass

    for q in range(CHUNKS):
        for t in range(1, 5):
            ring_step(q, t)
            if t == 3 and q + 1 < CHUNKS:
                ring_start(q + 1)
            if q == 0:
                prepare(t - 1)
            if q > 0 and t == 1:
                select(q - 1)
            if q > 0 and t == 4:
                if q < CHUNKS - 1:
                    stage1(q - 1)
                if q == 2:
                    for mm in range(OWN):
                        pacc[mm] = stage2(mm, 0)

    select(CHUNKS - 1)
    stage1(CHUNKS - 2)
    stage1(CHUNKS - 1)

    all_rows = lax.broadcasted_iota(jnp.int32, (NS, NS), 0)
    total = jnp.zeros((8, NS), F32)
    for mm in range(OWN):
        size = sizes_ref[group * MAC + piece * OWN + mm]
        product = jnp.where(all_rows < size, pacc[mm] + stage2(mm, 1), 0.0)
        total = total + jnp.sum(product.reshape(NS // 8, 8, NS), axis=0)
        pb[:, mm] = product.reshape(NSUB, 16, NS)
    sums[0] = total[:, :128] + total[:, 128:]

    tsub[piece] = sums[...]

    @pl.loop(1, NSUB)
    def _(offset):
        pltpu.make_async_remote_copy(
            src_ref=sums,
            dst_ref=tsub.at[piece],
            send_sem=tot_send.at[0],
            recv_sem=tot_recv.at[0],
            device_id=(group, sub_peer(offset)),
            device_id_type=MESH,
        ).start()

    @pl.loop(1, NSUB)
    def _(offset):
        j = sub_peer(offset)
        pltpu.make_async_remote_copy(
            src_ref=pb.at[j],
            dst_ref=out_ref.at[piece],
            send_sem=out_send,
            recv_sem=out_recv,
            device_id=(group, j),
            device_id_type=MESH,
        ).start()

    out_ref[piece] = pb[piece]
    pltpu.make_async_copy(tsub.at[pl.ds(0, NSUB - 1)], tsub.at[pl.ds(0, NSUB - 1)], tot_recv.at[0]).wait()
    tgrp[group] = jnp.sum(tsub[...], axis=0)

    @pl.loop(1, GROUPS)
    def _(offset):
        pltpu.make_async_remote_copy(
            src_ref=tgrp.at[group],
            dst_ref=tgrp.at[group],
            send_sem=tot_send.at[1],
            recv_sem=tot_recv.at[1],
            device_id=((group + offset) % GROUPS, piece),
            device_id_type=MESH,
        ).start()

    for q in range(CHUNKS):
        part = gathered[q].at[pl.ds(0, 14 * HALF)]
        pltpu.make_async_copy(part, part, ring_send.at[q]).wait()
        part = gathered[q].at[pl.ds(0, MAC + 14 * HALF)]
        pltpu.make_async_copy(part, part, d2d_send.at[q]).wait()
        part = outgo[q].at[pl.ds(0, NSUB - 1)]
        pltpu.make_async_copy(part, part, xy_send.at[q]).wait()
    part = tsub.at[pl.ds(0, NSUB - 1)]
    pltpu.make_async_copy(part, part, tot_send.at[0]).wait()
    live = jnp.sum(sizes_vec_ref[...].astype(F32)) * NS

    part = tgrp.at[pl.ds(0, GROUPS - 1)]
    pltpu.make_async_copy(part, part, tot_recv.at[1]).wait()
    both = jnp.sum(tgrp[...], axis=0)
    total, mass = jnp.sum(both[0]), jnp.sum(both[1])
    pick = lax.broadcasted_iota(jnp.int32, (8, 128), 0) == 0
    numer = jnp.where(pick, jnp.full((8, 128), live, F32), jnp.full((8, 128), total, F32))
    denom = jnp.where(pick, jnp.full((8, 128), total, F32), jnp.full((8, 128), mass, F32))
    stats_ref[...] = numer / denom

    pltpu.make_async_copy(part, part, tot_send.at[1]).wait()
    part = pb.at[pl.ds(0, NSUB - 1)]
    pltpu.make_async_copy(part, part, out_recv).wait()
    pltpu.make_async_copy(part, part, out_send).wait()


def on_device(
    macro_state, macro_sizes, block_sources, event_rates, first_factor, first_pattern, second_factor, second_pattern
):
    vmem, smem = pl.BlockSpec(memory_space=pltpu.VMEM), pl.BlockSpec(memory_space=pltpu.SMEM)
    dma = pltpu.SemaphoreType.DMA
    product, stats = pl.pallas_call(
        kernel,
        out_shape=(
            jax.ShapeDtypeStruct((NSUB, OWN, 16, NS), F32),
            jax.ShapeDtypeStruct((8, 128), F32),
        ),
        in_specs=[vmem, smem, vmem, smem, smem, vmem, vmem, vmem, vmem],
        out_specs=(vmem, vmem),
        scratch_shapes=[pltpu.VMEM((GROUPS * MAC, 8, 128), F32) for _ in range(CHUNKS)]
        + [pltpu.VMEM((NSUB, BLK, 8, 128), F32) for _ in range(2 * CHUNKS)]
        + [
            pltpu.VMEM((2, NS, EVENTS * 128), BF16),
            pltpu.VMEM((2, NS, EVENTS * 128), BF16),
            pltpu.VMEM((EVENTS, 2, 384, NS), BF16),
            pltpu.VMEM((EVENTS, NSUB * OWN * 8, NS), F32),
            pltpu.VMEM((OWN, EVENTS * 128, NS), BF16),
            pltpu.VMEM((OWN, EVENTS * 128, NS), BF16),
            pltpu.VMEM((OWN, NS, NS), F32),
            pltpu.VMEM((NSUB, OWN, 16, NS), F32),
            pltpu.VMEM((2, 8, 128), F32),
            pltpu.VMEM((NSUB, 2, 8, 128), F32),
            pltpu.VMEM((GROUPS, 2, 8, 128), F32),
            dma((CHUNKS,)),
            dma((CHUNKS * 16,)),
            dma((CHUNKS,)),
            dma((CHUNKS,)),
            dma((CHUNKS,)),
            dma((CHUNKS,)),
            dma((2,)),
            dma((2,)),
            dma,
            dma,
        ],
        compiler_params=pltpu.CompilerParams(
            collective_id=0, has_side_effects=True, vmem_limit_bytes=56 * 1024 * 1024
        ),
    )(
        macro_state,
        macro_sizes,
        macro_sizes.reshape(8, 128),
        block_sources.T,
        event_rates.T,
        first_factor,
        first_pattern,
        second_factor,
        second_pattern,
    )
    return product.reshape(MAC, 16, NS) * stats[0, 0], stats[1, 0]


def solution(mesh):
    return jax.shard_map(
        on_device,
        mesh=mesh,
        in_specs=(P("grp", "sub", None), P(), P(), P("grp", None), P(), P(), P(), P()),
        out_specs=(P("grp", "sub", None), P()),
        check_vma=False,
    )
```

time: 422 us -> 144 us (0.34)
  waiting for transfers between devices: 250 us -> 0 us
  Pallas kernels: 0 us -> 139 us
  blocking collectives: 75.6 us -> 0 us
  local copies, waits for them, and re-layouts: 29.6 us -> 1.32 us
  matrix products: 21.7 us -> 0 us
  between operations: 18.2 us -> 0.64 us
  other arithmetic: 15.9 us -> 2.92 us
  starting transfers between devices: 8.97 us -> 0 us
    pallas_call x0 -> x1, Pallas kernels: none -> 139 us  [on_device(): pl.pallas_call(kernel, out_shape=(jax.ShapeDtypeStruct((NSUB, OWN, 16, NS...]
    all_to_all x1 -> x0, waiting for transfers between devices: 137 us -> none  [on_device(): lax.all_to_all(outgoing, 'grp', split_axis=0, concat_axis=0, tiled=True)]
    reduce_scatter x1 -> x0, waiting for transfers between devices: 113 us -> none  [on_device(): lax.psum_scatter(jnp.einsum('kar,mkrc->amc', my_columns, scaled, precisio...]
    psum x1 -> x0, blocking collectives: 75.6 us -> none  [on_device(): total, mass = lax.psum((jnp.sum(product), jnp.sum(masked)), ('grp', 'sub'))]
    dot_general x2 -> x0, matrix products: 21.7 us -> none  [the longest x1 16.2 us: on_device(): jnp.einsum('kar,mkrc->amc', my_columns, scaled, precision=highest)]
    unnamed x25 -> x0, local copies, waits for them, and re-layouts: 17.2 us -> none
    gather x2 -> x0, local copies, waits for them, and re-layouts: 9.46 us -> none  [the longest x1 5.64 us: on_device(): stacked[my_from * capacity + my_slots]]
    another operation x2 -> x0, other arithmetic: 9.14 us -> none
  transfers between devices with their start and end apart: 2 -> 0, of which waited for: 2 -> 0; matrix products, arithmetic and copies ran while one was open for 1% -> 0% of each run, Pallas kernels for 0% -> 0%
where the time goes in v1:
time: 144 us; the launch traced here: 143 us
  Pallas kernels  139 us (97%)
  other arithmetic  2.92 us (2%)
    pallas_call x1, Pallas kernels, on_device(): pl.pallas_call(kernel, out_shape=(jax.ShapeDtypeStruct((NSUB, OWN, 16, NS...  139 us
    mul x1, other arithmetic, on_device(): return (product.reshape(MAC, 16, NS) * stats[0, 0], stats[1, 0])  2.92 us

profile of v1, /device:TPU:8, one launch (start us, length us, event | category | flops | bytes accessed | tf_op | source)
XLA Modules:
  0.0 143.4 jit_solution(6030053422123783816)
XLA Ops:
  0.6 138.5 %shard_map.95 = (f32[16,4,16,256]{3,2,1,0:T(8,128)}, f32[8,128]{1,0:T(8,128)}) custom-call(f32[64,16,256]{2,1,0:T(8,128)} %state_ref.1, s32[1024]{0:T(1024)} %sizes_ref.1, s32[8,128]{1,0:T(8,128)} %bitcast.8, s32[4,1024]{1,0:T(4,128)} %bitcast.7, f32[4,64]{1,0:T(4,128)} %bitcast.9, f32[4,256,256]{2,1,0:T(8,128)} %first_ref.1, s32[4,16,16]{2,1,0:T(8,128)} %fpat_ref.1, ...), custom_call_target="tpu_custom_call" | custom-call | tf_op jit(solution)/shard_map/pallas_call | solution.py:304
  139.2 1.3 fusion
  140.5 2.9 %broadcast_multiply_fusion = f32[16,4,16,256]{3,2,1,0:T(8,128)} fusion(f32[16,4,16,256]{3,2,1,0:T(8,128)} %get-tuple-element.4, f32[]{:T(128)} %bitcast.3), kind=kLoop, calls=%fused_computation | loop fusion | flops 262144 | bytes 2097156 | tf_op jit(solution)/shard_map/mul | solution.py:351

commit v2 on v1

--- a/solution.py
+++ b/solution.py
@@ -15,8 +15,10 @@
 OWN = MAC // NSUB
 BLK = OWN * EVENTS
 GROUPS = 2 * NZ
-HALF = MAC // 2
-CHUNKS = 4
+PAIRS = MAC // 2
+HALF = PAIRS // 2
+CHUNKS = 8
+STAGGER = 1.0
 CW, CCW = 0, 1
 
 
@@ -30,13 +32,16 @@
 
 
 def kernel(
-    state_ref, sizes_ref, sizes_vec_ref, sources_ref, rates_ref, first_ref, fpat_ref, second_ref, spat_ref,
+    state_hbm, sizes_hbm, sizes_vec_ref, sources_hbm, rates_hbm, first_hbm, fpat_hbm, second_hbm, spat_hbm,
     out_ref, stats_ref,
-    g0, g1, g2, g3, sb0, sb1, sb2, sb3, rb0, rb1, rb2, rb3,
-    fh, fl, stc, zacc, zh, zl, pacc, pb, sums, tsub, tgrp,
-    ring_send, ring_recv, d2d_send, d2d_recv, xy_send, xy_recv, tot_send, tot_recv, out_send, out_recv,
+    *scratch,
 ):
-    gathered, outgo, income = (g0, g1, g2, g3), (sb0, sb1, sb2, sb3), (rb0, rb1, rb2, rb3)
+    gathered, outgo, income = scratch[:CHUNKS], scratch[CHUNKS : 2 * CHUNKS], scratch[2 * CHUNKS : 3 * CHUNKS]
+    (
+        state_ref, sizes_ref, sources_ref, rates_ref, first_ref, fpat_ref, second_ref, spat_ref,
+        fh, fl, stc, zacc, zh, zl, pacc, pb, sums, tsub, tgrp,
+        load_sem, ring_send, ring_recv, d2d_send, d2d_recv, xy_send, xy_recv, tot_send, tot_recv, out_send, out_recv,
+    ) = scratch[3 * CHUNKS :]
     group, piece = lax.axis_index("grp"), lax.axis_index("sub")
     z, core = group // 2, group % 2
     y, x = piece // 4, piece % 4
@@ -58,22 +63,45 @@
     def _(offset):
         pl.semaphore_signal(barrier, inc=1, device_id=((group + offset) % GROUPS, piece), device_id_type=MESH)
 
+    loads = [
+        pltpu.make_async_copy(source, dest, load_sem.at[i])
+        for i, (source, dest) in enumerate(
+            (
+                (state_hbm, state_ref),
+                (sizes_hbm, sizes_ref),
+                (sources_hbm, sources_ref),
+                (rates_hbm, rates_ref),
+                (first_hbm, first_ref),
+                (fpat_hbm, fpat_ref),
+                (second_hbm, second_ref),
+                (spat_hbm, spat_ref),
+            )
+        )
+    ]
+    for load in loads:
+        load.start()
+
     row_iota = lax.broadcasted_iota(jnp.int32, (8, 128), 0)
-
-    def stage(q, mass):
-        rh, ch = q // 2, q % 2
+    low_lanes = lax.broadcasted_iota(jnp.int32, (8, 128), 1) < 64
+
+    def stage(rh, ch, mass):
         rows = row_iota + (piece * 16 + rh * 8)
-
-        def body(m, mass):
+        q = rh * 4 + ch * 2
+
+        def masked(m):
             tile = state_ref[m, pl.ds(8 * rh, 8), pl.ds(128 * ch, 128)]
-            tile = jnp.where(rows < sizes_ref[group * MAC + m], tile, 0.0)
-            gathered[q][group * MAC + m] = tile
-            return mass + tile
-
-        return lax.fori_loop(0, MAC, body, mass, unroll=8)
+            return jnp.where(rows < sizes_ref[group * MAC + m], tile, 0.0)
+
+        def body(p, mass):
+            even, odd = masked(2 * p), masked(2 * p + 1)
+            gathered[q][group * PAIRS + p] = jnp.where(low_lanes, even, pltpu.roll(odd, 64, 1))
+            gathered[q + 1][group * PAIRS + p] = jnp.where(low_lanes, pltpu.roll(even, 64, 1), odd)
+            return mass + even + odd
+
+        return lax.fori_loop(0, PAIRS, body, mass, unroll=8)
 
     def ring_piece(q, distance, h):
-        return gathered[q].at[pl.ds(ring_group(distance) * MAC + HALF * h, HALF)]
+        return gathered[q].at[pl.ds(ring_group(distance) * PAIRS + HALF * h, HALF)]
 
     def ring_copy(q, way, t, h):
         sign = -1 if way == CW else 1
@@ -109,7 +137,7 @@
         for h in (0, 1):
             for way in (CW, CCW):
                 ring_copy(q, way, 1, h).start()
-        sibling_copy(q, gathered[q].at[pl.ds(group * MAC, MAC)])
+        sibling_copy(q, gathered[q].at[pl.ds(group * PAIRS, PAIRS)])
 
     def ring_step(q, t):
         for h in (0, 1):
@@ -138,21 +166,30 @@
             for rh in (0, 1):
                 dest[rh, :, k * 128 : (k + 1) * 128] = moved[:, rh * 128 : (rh + 1) * 128]
         high, low = split((second_ref[k] * widen(spat_ref[k])).T)
-        for ch in (0, 1):
-            rows = slice(ch * 128, ch * 128 + 128)
-            stc[k, ch, 0:128, :] = high[rows]
-            stc[k, ch, 128:256, :] = low[rows]
-            stc[k, ch, 256:384, :] = high[rows]
+        zeros = jnp.zeros((64, NS), BF16)
+        for cq in range(4):
+            rows = slice(cq * 64, cq * 64 + 64)
+            for third, part in enumerate((high[rows], low[rows], high[rows])):
+                at = third * 128
+                stc[k, cq, at : at + 64, :NS] = part
+                stc[k, cq, at : at + 64, NS:] = zeros
+                stc[k, cq, at + 64 : at + 128, :NS] = zeros
+                stc[k, cq, at + 64 : at + 128, NS:] = part
 
     def select(q):
-        pltpu.make_async_copy(
-            gathered[q].at[pl.ds(0, 512)], gathered[q].at[pl.ds(0, 512)], d2d_recv.at[q]
-        ).wait()
+        part = gathered[q].at[pl.ds(0, GROUPS // 2 * PAIRS)]
+        pltpu.make_async_copy(part, part, d2d_recv.at[q]).wait()
 
         def pick(j, dest, at):
-            tiles = [
-                gathered[q][sources_ref[k, group * MAC + j * OWN + mm]] for k in range(EVENTS) for mm in range(OWN)
-            ]
+            tiles = []
+            for k in range(EVENTS):
+                for u in range(OWN // 2):
+                    even = sources_ref[k, group * MAC + j * OWN + 2 * u]
+                    odd = sources_ref[k, group * MAC + j * OWN + 2 * u + 1]
+                    one, two = gathered[q][even // 2], gathered[q][odd // 2]
+                    one = jnp.where(even % 2 == 0, one, pltpu.roll(one, 64, 1))
+                    two = jnp.where(odd % 2 == 0, pltpu.roll(two, 64, 1), two)
+                    tiles.append(jnp.where(low_lanes, one, two))
             for b, tile in enumerate(tiles):
                 dest[at, b] = tile
 
@@ -172,21 +209,22 @@
         pick(piece, income[q], piece)
 
     def stage1(q):
-        rh, ch = q // 2, q % 2
-        pltpu.make_async_copy(
-            income[q].at[pl.ds(0, NSUB - 1)], income[q].at[pl.ds(0, NSUB - 1)], xy_recv.at[q]
-        ).wait()
+        rh, cq = q // 4, q % 4
+        part = income[q].at[pl.ds(0, NSUB - 1)]
+        pltpu.make_async_copy(part, part, xy_recv.at[q]).wait()
         for k in range(EVENTS):
-            block = income[q][:, k * OWN : (k + 1) * OWN].reshape(NSUB * OWN * 8, 128)
+            block = income[q][:, k * OWN // 2 : (k + 1) * OWN // 2].reshape(NSUB * OWN // 2 * 8, 128)
             high, low = split(block)
-            part = dot(jnp.concatenate([high, high, low], axis=1), stc[k, ch])
-            if ch == 0:
+            part = dot(jnp.concatenate([high, high, low], axis=1), stc[k, cq])
+            if cq > 0:
+                part = part + zacc[k]
+            if cq < 3:
                 zacc[k] = part
             else:
-                part = (part + zacc[k]).reshape(NSUB, OWN, 8, NS)
                 for mm in range(OWN):
                     rate = rates_ref[k, piece * OWN + mm]
-                    high, low = split(part[:, mm].reshape(128, NS) * rate)
+                    half = part[:, mm % 2 * NS : mm % 2 * NS + NS].reshape(NSUB, OWN // 2, 8, NS)
+                    high, low = split(half[:, mm // 2].reshape(128, NS) * rate)
                     zh[mm, k * 128 : (k + 1) * 128, :] = high
                     zl[mm, k * 128 : (k + 1) * 128, :] = low
 
@@ -194,28 +232,36 @@
         high, low = zh[mm], zl[mm]
         return dot(fh[rh], high) + dot(fh[rh], low) + dot(fl[rh], high)
 
-    mass = stage(0, jnp.zeros((8, 128), F32))
+    loads[0].wait()
+    loads[1].wait()
+    mass = stage(0, 0, jnp.zeros((8, 128), F32))
     pl.semaphore_wait(barrier, NSUB - 1 + GROUPS - 1)
     ring_start(0)
-    for q in range(1, CHUNKS):
-        mass = stage(q, mass)
-    sums[1] = mass
-
-    for q in range(CHUNKS):
-        for t in range(1, 5):
-            ring_step(q, t)
-            if t == 3 and q + 1 < CHUNKS:
-                ring_start(q + 1)
-            if q == 0:
-                prepare(t - 1)
-            if q > 0 and t == 1:
-                select(q - 1)
-            if q > 0 and t == 4:
-                if q < CHUNKS - 1:
-                    stage1(q - 1)
-                if q == 2:
-                    for mm in range(OWN):
-                        pacc[mm] = stage2(mm, 0)
+    mass = stage(0, 1, mass)
+
+    events = sorted((q * STAGGER + t, q, t) for q in range(CHUNKS) for t in range(1, 5))
+    started, due, todo = 1, [], list(range(EVENTS))
+    for now, q, t in events:
+        while started < CHUNKS and started * STAGGER <= now - 1:
+            ring_start(started)
+            started += 1
+        ring_step(q, t)
+        if (q, t) == (0, 1):
+            mass = stage(1, 0, mass)
+            mass = stage(1, 1, mass)
+            sums[1] = mass
+            for load in loads[2:]:
+                load.wait()
+        elif todo:
+            prepare(todo.pop(0))
+        for task in due:
+            select(task)
+            if task > 0:
+                stage1(task - 1)
+            if task == 4:
+                for mm in range(OWN):
+                    pacc[mm] = stage2(mm, 0)
+        due = [q] if t == 4 else []
 
     select(CHUNKS - 1)
     stage1(CHUNKS - 2)
@@ -273,7 +319,7 @@
     for q in range(CHUNKS):
         part = gathered[q].at[pl.ds(0, 14 * HALF)]
         pltpu.make_async_copy(part, part, ring_send.at[q]).wait()
-        part = gathered[q].at[pl.ds(0, MAC + 14 * HALF)]
+        part = gathered[q].at[pl.ds(0, PAIRS + 14 * HALF)]
         pltpu.make_async_copy(part, part, d2d_send.at[q]).wait()
         part = outgo[q].at[pl.ds(0, NSUB - 1)]
         pltpu.make_async_copy(part, part, xy_send.at[q]).wait()
@@ -296,26 +342,39 @@
     pltpu.make_async_copy(part, part, out_send).wait()
 
 
+def rescale(product_ref, stats_ref, scaled_ref, growth_ref):
+    scaled_ref[...] = product_ref[...] * stats_ref[0:1, 0:1].reshape(1, 1, 1)
+    growth_ref[...] = stats_ref[1:2, 0:1]
+
+
 def on_device(
     macro_state, macro_sizes, block_sources, event_rates, first_factor, first_pattern, second_factor, second_pattern
 ):
-    vmem, smem = pl.BlockSpec(memory_space=pltpu.VMEM), pl.BlockSpec(memory_space=pltpu.SMEM)
+    vmem, hbm = pl.BlockSpec(memory_space=pltpu.VMEM), pl.BlockSpec(memory_space=pltpu.HBM)
     dma = pltpu.SemaphoreType.DMA
     product, stats = pl.pallas_call(
         kernel,
         out_shape=(
-            jax.ShapeDtypeStruct((NSUB, OWN, 16, NS), F32),
-            jax.ShapeDtypeStruct((8, 128), F32),
+            pltpu.VMEM((NSUB, OWN, 16, NS), F32),
+            pltpu.VMEM((8, 128), F32),
         ),
-        in_specs=[vmem, smem, vmem, smem, smem, vmem, vmem, vmem, vmem],
+        in_specs=[hbm, hbm, vmem, hbm, hbm, hbm, hbm, hbm, hbm],
         out_specs=(vmem, vmem),
-        scratch_shapes=[pltpu.VMEM((GROUPS * MAC, 8, 128), F32) for _ in range(CHUNKS)]
-        + [pltpu.VMEM((NSUB, BLK, 8, 128), F32) for _ in range(2 * CHUNKS)]
+        scratch_shapes=[pltpu.VMEM((GROUPS * PAIRS, 8, 128), F32) for _ in range(CHUNKS)]
+        + [pltpu.VMEM((NSUB, BLK // 2, 8, 128), F32) for _ in range(2 * CHUNKS)]
         + [
+            pltpu.VMEM((MAC, 16, NS), F32),
+            pltpu.SMEM((GROUPS * MAC,), jnp.int32),
+            pltpu.SMEM((EVENTS, GROUPS * MAC), jnp.int32),
+            pltpu.SMEM((EVENTS, MAC), F32),
+            pltpu.VMEM((EVENTS, NS, NS), F32),
+            pltpu.VMEM((EVENTS, 16, 16), jnp.int32),
+            pltpu.VMEM((EVENTS, NS, NS), F32),
+            pltpu.VMEM((EVENTS, 16, 16), jnp.int32),
             pltpu.VMEM((2, NS, EVENTS * 128), BF16),
             pltpu.VMEM((2, NS, EVENTS * 128), BF16),
-            pltpu.VMEM((EVENTS, 2, 384, NS), BF16),
-            pltpu.VMEM((EVENTS, NSUB * OWN * 8, NS), F32),
+            pltpu.VMEM((EVENTS, 4, 384, 2 * NS), BF16),
+            pltpu.VMEM((EVENTS, NSUB * OWN // 2 * 8, 2 * NS), F32),
             pltpu.VMEM((OWN, EVENTS * 128, NS), BF16),
             pltpu.VMEM((OWN, EVENTS * 128, NS), BF16),
             pltpu.VMEM((OWN, NS, NS), F32),
@@ -323,6 +382,7 @@
             pltpu.VMEM((2, 8, 128), F32),
             pltpu.VMEM((NSUB, 2, 8, 128), F32),
             pltpu.VMEM((GROUPS, 2, 8, 128), F32),
+            dma((8,)),
             dma((CHUNKS,)),
             dma((CHUNKS * 16,)),
             dma((CHUNKS,)),
@@ -348,7 +408,19 @@
         second_factor,
         second_pattern,
     )
-    return product.reshape(MAC, 16, NS) * stats[0, 0], stats[1, 0]
+    scaled, growth = pl.pallas_call(
+        rescale,
+        out_shape=(
+            jax.ShapeDtypeStruct((MAC, 16, NS), F32),
+            jax.ShapeDtypeStruct((1, 1), F32),
+        ),
+        in_specs=[vmem, vmem],
+        out_specs=(vmem, vmem),
+    )(
+        pltpu.with_memory_space_constraint(product.reshape(MAC, 16, NS), pltpu.VMEM),
+        pltpu.with_memory_space_constraint(stats, pltpu.VMEM),
+    )
+    return scaled, growth.reshape(())
 
 
 def solution(mesh):

time: 144 us -> 131 us (0.910)
  Pallas kernels: 139 us -> 130 us
  other arithmetic: 2.92 us -> 0 us
    pallas_call x1 -> x2, Pallas kernels: 139 us -> 130 us  [the longest x1 129 us: on_device(): pl.pallas_call(kernel, out_shape=(pltpu.VMEM((NSUB, OWN, 16, NS), F32), p...]
    mul x1 -> x0, other arithmetic: 2.92 us -> none  [on_device(): return (product.reshape(MAC, 16, NS) * stats[0, 0], stats[1, 0])]
where the time goes in v2:
time: 131 us
  Pallas kernels  130 us (99%)
    pallas_call x1, Pallas kernels, on_device(): pl.pallas_call(kernel, out_shape=(pltpu.VMEM((NSUB, OWN, 16, NS), F32), p...  129 us

profile of v2, /device:TPU:8, one launch (start us, length us, event | category | flops | bytes accessed | tf_op | source)
XLA Modules:
  0.0 130.7 jit_solution(632247611958880219)
XLA Ops:
  0.6 128.9 %shard_map.95 = (f32[16,4,16,256]{3,2,1,0:T(8,128)S(1)}, f32[8,128]{1,0:T(8,128)S(1)}) custom-call(f32[64,16,256]{2,1,0:T(8,128)} %state_hbm.1, s32[1024]{0:T(1024)} %sizes_hbm.1, s32[8,128]{1,0:T(8,128)} %bitcast.7, s32[4,1024]{1,0:T(4,128)} %bitcast.6, f32[4,64]{1,0:T(4,128)} %bitcast.8, f32[4,256,256]{2,1,0:T(8,128)} %first_hbm.1, s32[4,16,16]{2,1,0:T(8,128)} %fpat_hbm.1, ...), custom_call_target="tpu_custom_call" | custom-call | tf_op jit(solution)/shard_map/pallas_call | solution.py:355
  129.6 1.1 shard_map.96

commit v3 on v2

--- a/solution.py
+++ b/solution.py
@@ -1,3 +1,5 @@
+import functools
+
 import jax
 import jax.numpy as jnp
 from jax import lax
@@ -18,6 +20,9 @@
 PAIRS = MAC // 2
 HALF = PAIRS // 2
 CHUNKS = 8
+DELAY = 2
+LAG = 6
+BURST = 1
 STAGGER = 1.0
 CW, CCW = 0, 1
 
@@ -176,9 +181,10 @@
                 stc[k, cq, at + 64 : at + 128, :NS] = zeros
                 stc[k, cq, at + 64 : at + 128, NS:] = part
 
-    def select(q):
-        part = gathered[q].at[pl.ds(0, GROUPS // 2 * PAIRS)]
-        pltpu.make_async_copy(part, part, d2d_recv.at[q]).wait()
+    def select(q, first, last):
+        if first == 1:
+            part = gathered[q].at[pl.ds(0, GROUPS // 2 * PAIRS)]
+            pltpu.make_async_copy(part, part, d2d_recv.at[q]).wait()
 
         def pick(j, dest, at):
             tiles = []
@@ -186,14 +192,13 @@
                 for u in range(OWN // 2):
                     even = sources_ref[k, group * MAC + j * OWN + 2 * u]
                     odd = sources_ref[k, group * MAC + j * OWN + 2 * u + 1]
-                    one, two = gathered[q][even // 2], gathered[q][odd // 2]
-                    one = jnp.where(even % 2 == 0, one, pltpu.roll(one, 64, 1))
-                    two = jnp.where(odd % 2 == 0, pltpu.roll(two, 64, 1), two)
+                    one = pltpu.roll(gathered[q][lax.shift_right_logical(even, 1)], (even & 1) * 64, 1)
+                    two = pltpu.roll(gathered[q][lax.shift_right_logical(odd, 1)], 64 - (odd & 1) * 64, 1)
                     tiles.append(jnp.where(low_lanes, one, two))
             for b, tile in enumerate(tiles):
                 dest[at, b] = tile
 
-        @pl.loop(1, NSUB)
+        @pl.loop(first, last)
         def _(offset):
             j = sub_peer(offset)
             pick(j, outgo[q], j)
@@ -206,13 +211,15 @@
                 device_id_type=MESH,
             ).start()
 
-        pick(piece, income[q], piece)
-
-    def stage1(q):
+        if last == NSUB:
+            pick(piece, income[q], piece)
+
+    def stage1(q, events):
         rh, cq = q // 4, q % 4
-        part = income[q].at[pl.ds(0, NSUB - 1)]
-        pltpu.make_async_copy(part, part, xy_recv.at[q]).wait()
-        for k in range(EVENTS):
+        if events[0] == 0:
+            part = income[q].at[pl.ds(0, NSUB - 1)]
+            pltpu.make_async_copy(part, part, xy_recv.at[q]).wait()
+        for k in events:
             block = income[q][:, k * OWN // 2 : (k + 1) * OWN // 2].reshape(NSUB * OWN // 2 * 8, 128)
             high, low = split(block)
             part = dot(jnp.concatenate([high, high, low], axis=1), stc[k, cq])
@@ -239,33 +246,41 @@
     ring_start(0)
     mass = stage(0, 1, mass)
 
-    events = sorted((q * STAGGER + t, q, t) for q in range(CHUNKS) for t in range(1, 5))
-    started, due, todo = 1, [], list(range(EVENTS))
-    for now, q, t in events:
+    def finish_stage(mass):
+        mass = stage(1, 1, stage(1, 0, mass))
+        sums[1] = mass
+        for load in loads[2:]:
+            load.wait()
+
+    def first_product(mm):
+        pacc[mm] = stage2(mm, 0)
+
+    picks, products = [], [(0, functools.partial(prepare, k)) for k in range(EVENTS)]
+    started = 1
+    steps = sorted((q * STAGGER + t, q, t) for q in range(CHUNKS) for t in range(1, 5))
+    for at, (now, q, t) in enumerate(steps):
         while started < CHUNKS and started * STAGGER <= now - 1:
             ring_start(started)
             started += 1
         ring_step(q, t)
-        if (q, t) == (0, 1):
-            mass = stage(1, 0, mass)
-            mass = stage(1, 1, mass)
-            sums[1] = mass
-            for load in loads[2:]:
-                load.wait()
-        elif todo:
-            prepare(todo.pop(0))
-        for task in due:
-            select(task)
-            if task > 0:
-                stage1(task - 1)
-            if task == 4:
-                for mm in range(OWN):
-                    pacc[mm] = stage2(mm, 0)
-        due = [q] if t == 4 else []
-
-    select(CHUNKS - 1)
-    stage1(CHUNKS - 2)
-    stage1(CHUNKS - 1)
+        if at == 0:
+            finish_stage(mass)
+            continue
+        for _ in range(BURST):
+            for queue in (picks, products):
+                if queue and queue[0][0] <= at:
+                    queue.pop(0)[1]()
+                    break
+        if t == 4:
+            picks.append((at + DELAY, functools.partial(select, q, 1, NSUB // 2)))
+            picks.append((at + DELAY, functools.partial(select, q, NSUB // 2, NSUB)))
+            products.append((at + DELAY + LAG, functools.partial(stage1, q, (0, 1))))
+            products.append((at + DELAY + LAG, functools.partial(stage1, q, (2, 3))))
+            if q == 3:
+                products.extend((0, functools.partial(first_product, mm)) for mm in range(OWN))
+
+    for _, task in picks + products:
+        task()
 
     all_rows = lax.broadcasted_iota(jnp.int32, (NS, NS), 0)
     total = jnp.zeros((8, NS), F32)

time: 131 us -> 127 us (0.969)
  Pallas kernels: 130 us -> 126 us
    pallas_call x1, Pallas kernels: 129 us -> 125 us  [on_device(): pl.pallas_call(kernel, out_shape=(pltpu.VMEM((NSUB, OWN, 16, NS), F32), p...]
where the time goes in v3:
time: 127 us
  Pallas kernels  126 us (99%)
    pallas_call x1, Pallas kernels, on_device(): pl.pallas_call(kernel, out_shape=(pltpu.VMEM((NSUB, OWN, 16, NS), F32), p...  125 us

profile of v3, /device:TPU:8, one launch (start us, length us, event | category | flops | bytes accessed | tf_op | source)
XLA Modules:
  0.0 126.5 jit_solution(18218076267404677917)
XLA Ops:
  0.6 124.8 %shard_map.95 = (f32[16,4,16,256]{3,2,1,0:T(8,128)S(1)}, f32[8,128]{1,0:T(8,128)S(1)}) custom-call(f32[64,16,256]{2,1,0:T(8,128)} %state_hbm.1, s32[1024]{0:T(1024)} %sizes_hbm.1, s32[8,128]{1,0:T(8,128)} %bitcast.7, s32[4,1024]{1,0:T(4,128)} %bitcast.6, f32[4,64]{1,0:T(4,128)} %bitcast.8, f32[4,256,256]{2,1,0:T(8,128)} %first_hbm.1, s32[4,16,16]{2,1,0:T(8,128)} %fpat_hbm.1, ...), custom_call_target="tpu_custom_call" | custom-call | tf_op jit(solution)/shard_map/pallas_call | solution.py:370
  125.4 1.1 shard_map.96

commit v4 on v3

--- a/solution.py
+++ b/solution.py
@@ -151,7 +151,10 @@
                     ring_wait(q, way, t, h)
                     if t < 4 and h in carried(way, t + 1):
                         ring_copy(q, way, t + 1, h).start()
-                    sibling_copy(q, ring_piece(q, -t if way == CW else t, h))
+                    if t == 4:
+                        sibling_copy(q, ring_piece(q, -t if way == CW else t, h))
+                    elif h == 1:
+                        sibling_copy(q, gathered[q].at[pl.ds(ring_group(-t if way == CW else t) * PAIRS, PAIRS)])
 
     def prepare(k):
         rows_of = (lax.broadcasted_iota(jnp.int32, (NS, 16), 0) // 16 == lax.broadcasted_iota(jnp.int32, (NS, 16), 1))
@@ -248,7 +251,7 @@
 
     def finish_stage(mass):
         mass = stage(1, 1, stage(1, 0, mass))
-        sums[1] = mass
+        sums[1:2, :] = jnp.sum(mass, axis=0, keepdims=True)
         for load in loads[2:]:
             load.wait()
 
@@ -289,7 +292,7 @@
         product = jnp.where(all_rows < size, pacc[mm] + stage2(mm, 1), 0.0)
         total = total + jnp.sum(product.reshape(NS // 8, 8, NS), axis=0)
         pb[:, mm] = product.reshape(NSUB, 16, NS)
-    sums[0] = total[:, :128] + total[:, 128:]
+    sums[0:1, :] = jnp.sum(total[:, :128] + total[:, 128:], axis=0, keepdims=True)
 
     tsub[piece] = sums[...]
 
@@ -345,7 +348,7 @@
     part = tgrp.at[pl.ds(0, GROUPS - 1)]
     pltpu.make_async_copy(part, part, tot_recv.at[1]).wait()
     both = jnp.sum(tgrp[...], axis=0)
-    total, mass = jnp.sum(both[0]), jnp.sum(both[1])
+    total, mass = jnp.sum(both[0:1]), jnp.sum(both[1:2])
     pick = lax.broadcasted_iota(jnp.int32, (8, 128), 0) == 0
     numer = jnp.where(pick, jnp.full((8, 128), live, F32), jnp.full((8, 128), total, F32))
     denom = jnp.where(pick, jnp.full((8, 128), total, F32), jnp.full((8, 128), mass, F32))
@@ -394,9 +397,9 @@
             pltpu.VMEM((OWN, EVENTS * 128, NS), BF16),
             pltpu.VMEM((OWN, NS, NS), F32),
             pltpu.VMEM((NSUB, OWN, 16, NS), F32),
-            pltpu.VMEM((2, 8, 128), F32),
-            pltpu.VMEM((NSUB, 2, 8, 128), F32),
-            pltpu.VMEM((GROUPS, 2, 8, 128), F32),
+            pltpu.VMEM((2, 128), F32),
+            pltpu.VMEM((NSUB, 2, 128), F32),
+            pltpu.VMEM((GROUPS, 2, 128), F32),
             dma((8,)),
             dma((CHUNKS,)),
             dma((CHUNKS * 16,)),

time: 127 us -> 126 us (level)
  no operation moved by 1% of the time
where the time goes in v4:
time: 126 us
  Pallas kernels  125 us (99%)
    pallas_call x1, Pallas kernels, on_device(): pl.pallas_call(kernel, out_shape=(pltpu.VMEM((NSUB, OWN, 16, NS), F32), p...  124 us

profile of v4, /device:TPU:8, one launch (start us, length us, event | category | flops | bytes accessed | tf_op | source)
XLA Modules:
  0.0 125.6 jit_solution(1258998190751866354)
XLA Ops:
  0.6 123.9 %shard_map.95 = (f32[16,4,16,256]{3,2,1,0:T(8,128)S(1)}, f32[8,128]{1,0:T(8,128)S(1)}) custom-call(f32[64,16,256]{2,1,0:T(8,128)} %state_hbm.1, s32[1024]{0:T(1024)} %sizes_hbm.1, s32[8,128]{1,0:T(8,128)} %bitcast.7, s32[4,1024]{1,0:T(4,128)} %bitcast.6, f32[4,64]{1,0:T(4,128)} %bitcast.8, f32[4,256,256]{2,1,0:T(8,128)} %first_hbm.1, s32[4,16,16]{2,1,0:T(8,128)} %fpat_hbm.1, ...), custom_call_target="tpu_custom_call" | custom-call | tf_op jit(solution)/shard_map/pallas_call | solution.py:373
  124.5 1.1 shard_map.96

commit v5 on v4

--- a/solution.py
+++ b/solution.py
@@ -60,13 +60,13 @@
 
     barrier = pltpu.get_barrier_semaphore()
 
+    @pl.loop(1, GROUPS)
+    def _(offset):
+        pl.semaphore_signal(barrier, inc=1, device_id=((group + offset) % GROUPS, piece), device_id_type=MESH)
+
     @pl.loop(1, NSUB)
     def _(offset):
         pl.semaphore_signal(barrier, inc=1, device_id=(group, sub_peer(offset)), device_id_type=MESH)
-
-    @pl.loop(1, GROUPS)
-    def _(offset):
-        pl.semaphore_signal(barrier, inc=1, device_id=((group + offset) % GROUPS, piece), device_id_type=MESH)
 
     loads = [
         pltpu.make_async_copy(source, dest, load_sem.at[i])

time: 126 us -> 126 us (level)
  no operation moved by 1% of the time
where the time goes in v5:
time: 126 us
  Pallas kernels  125 us (99%)
    pallas_call x1, Pallas kernels, on_device(): pl.pallas_call(kernel, out_shape=(pltpu.VMEM((NSUB, OWN, 16, NS), F32), p...  124 us

profile of v5, /device:TPU:8, one launch (start us, length us, event | category | flops | bytes accessed | tf_op | source)
XLA Modules:
  0.0 125.5 jit_solution(228989554814812722)
XLA Ops:
  0.6 123.8 %shard_map.95 = (f32[16,4,16,256]{3,2,1,0:T(8,128)S(1)}, f32[8,128]{1,0:T(8,128)S(1)}) custom-call(f32[64,16,256]{2,1,0:T(8,128)} %state_hbm.1, s32[1024]{0:T(1024)} %sizes_hbm.1, s32[8,128]{1,0:T(8,128)} %bitcast.7, s32[4,1024]{1,0:T(4,128)} %bitcast.6, f32[4,64]{1,0:T(4,128)} %bitcast.8, f32[4,256,256]{2,1,0:T(8,128)} %first_hbm.1, s32[4,16,16]{2,1,0:T(8,128)} %fpat_hbm.1, ...), custom_call_target="tpu_custom_call" | custom-call | tf_op jit(solution)/shard_map/pallas_call | solution.py:373
  124.5 1.1 shard_map.96
